TPU v7x, 1024 devices: a whole 4x4x32 slice. The times are simulated.
1024 devices in a mesh: grp: 8 (over x, core), blk: 32 (over z), rep: 4 (over y).
Axes of the slice: x: 4, y: 4, z: 32, core: 2. Of those that a mesh axis runs over, the one named last changes fastest.
Arguments:
- tod: float32 [8192, 1024], P(('grp', 'blk', 'rep')), may hold values from -6 to 6
- hit_ids: int32 [256, 32, 8], P(('grp', 'blk')), may hold values from 0 to 255
- sample_slot: int32 [8192, 1024], P(('grp', 'blk', 'rep')), may hold values from 0 to 255
- sample_offset: int32 [8192, 1024], P(('grp', 'blk', 'rep')), may hold values from 0 to 127
- prior: float32 [8192, 9], P(('grp', 'blk', 'rep')), may hold values from 0.5 to 8
Outputs:
- offset_amplitudes_iterate: float32 [8192, 16], P(('grp', 'blk', 'rep'))
- leftover_error: float32 [8192, 16], P(('grp', 'blk', 'rep'))
Inputs may be any that keep to these rules, and one draw needn't show every extreme that they name: `hit_ids`: A block of the list at owner o is one of owner o's blocks. `sample_slot`: entry s of a list belongs to owner s // 8.
All inputs are finite; a program needn't handle non-finite values.
Results may differ from a plain program's by a relative error of at most 0.0003.
Values sent between devices are 32-bit elements; how exact they have to be, the bound alone decides.
A program may use at most 32 MiB of HBM per device.

v0:
```python
import math

import jax
import jax.numpy as jnp
from jax import lax
from jax.sharding import PartitionSpec as P

BL = 64
OWN = 256
ITERS = 3


def filtered(value_entries, prior):
    length = value_entries.shape[1]
    freqs = prior.shape[1]
    sample_position_index = lax.broadcasted_iota(jnp.int32, (length, freqs), 0)
    freq_index = lax.broadcasted_iota(jnp.int32, (length, freqs), 1)
    angles = (
        2.0 * math.pi / length * (sample_position_index * freq_index % length).astype(jnp.float32)
    )
    cosine_terms = jnp.cos(angles)
    sines = jnp.sin(angles)
    border = (freq_index == 0) | (2 * freq_index == length)
    weights = jnp.where(border, 1.0, 2.0) / length
    highest = lax.Precision.HIGHEST
    real_component = jnp.dot(
        value_entries, cosine_terms, precision=highest, preferred_element_type=jnp.float32
    )
    imag_part = jnp.dot(value_entries, sines, precision=highest, preferred_element_type=jnp.float32)
    first = jnp.dot(
        prior * real_component,
        (cosine_terms * weights).T,
        precision=highest,
        preferred_element_type=jnp.float32,
    )
    second = jnp.dot(
        prior * imag_part,
        (sines * weights).T,
        precision=highest,
        preferred_element_type=jnp.float32,
    )
    return first + second


def shards(tod, hit_ids, sample_slot, sample_offset, prior):
    detectors, samples = tod.shape
    owners = hit_ids.shape[1]
    per_owner = hit_ids.shape[2]
    local_index = (sample_slot * 128 + sample_offset).reshape(-1)
    slot_ids = hit_ids[0]

    def bin_one(flat_field):
        return jax.ops.segment_sum(flat_field, local_index, num_segments=owners * per_owner * 128)

    def project(fields):
        field_count = fields.shape[0]
        binned_rows = jnp.stack(
            [bin_one(fields[index].reshape(-1)) for index in range(field_count)]
        )
        partial_value = binned_rows.reshape(field_count, owners, per_owner, 128).transpose(
            1, 2, 0, 3
        )
        received, received_ids = (
            lax.all_to_all(partial_value, "blk", split_axis=0, concat_axis=0, tiled=True),
            lax.all_to_all(slot_ids, "blk", split_axis=0, concat_axis=0, tiled=True),
        )
        segment = jax.ops.segment_sum(
            received.reshape(-1, field_count, 128), received_ids.reshape(-1), num_segments=OWN
        )
        return (lax.psum(segment, ("grp", "rep")), received_ids)

    def read_back(block_map, received_ids):
        wanted = block_map[received_ids]
        returned = lax.all_to_all(wanted, "blk", split_axis=0, concat_axis=0, tiled=True)
        return returned.reshape(-1)[local_index].reshape(detectors, samples)

    def folded(signal):
        return signal.reshape(detectors, -1, BL).sum(axis=2)

    totals, first_ids = project(jnp.stack([tod, jnp.ones_like(tod)]))
    divisor = jnp.maximum(totals[:, 1], 1.0)
    source_array = folded(tod - read_back(totals[:, 0] / divisor, first_ids))

    def operate(value_entries):
        signal = jnp.broadcast_to(
            value_entries[:, :, None], (detectors, value_entries.shape[1], BL)
        ).reshape(detectors, samples)
        sums_now, ids_now = project(signal[None])
        cleaned = signal - read_back(sums_now[:, 0] / divisor, ids_now)
        return folded(cleaned) + filtered(value_entries, prior)

    def pairwise_inner(leftover_error, image):
        return lax.psum(
            (jnp.sum(leftover_error * leftover_error), jnp.sum(leftover_error * image)),
            ("grp", "blk", "rep"),
        )

    offset_amplitudes_iterate = jnp.zeros_like(source_array)
    leftover_error = source_array
    image = operate(leftover_error)
    norm_now, curvature = pairwise_inner(leftover_error, image)
    descent_factor = norm_now / curvature
    update_course, along = (leftover_error, image)
    for iteration in range(ITERS):
        offset_amplitudes_iterate = offset_amplitudes_iterate + descent_factor * update_course
        leftover_error = leftover_error - descent_factor * along
        if iteration + 1 < ITERS:
            image = operate(leftover_error)
            following_squared_magnitude, curvature = pairwise_inner(leftover_error, image)
            factor = following_squared_magnitude / norm_now
            descent_factor = following_squared_magnitude / (
                curvature - factor * following_squared_magnitude / descent_factor
            )
            update_course = leftover_error + factor * update_course
            along = image + factor * along
            norm_now = following_squared_magnitude
    return (offset_amplitudes_iterate, leftover_error)


def solution(mesh):
    in_specs = (
        P(("grp", "blk", "rep"), None),
        P(("grp", "blk"), None, None),
        P(("grp", "blk", "rep"), None),
        P(("grp", "blk", "rep"), None),
        P(("grp", "blk", "rep"), None),
    )
    out_specs = (P(("grp", "blk", "rep"), None), P(("grp", "blk", "rep"), None))
    return jax.shard_map(shards, mesh=mesh, in_specs=in_specs, out_specs=out_specs, check_vma=False)
```

profile of v0, /device:TPU:1, one launch (start us, length us, event | category | flops | bytes accessed | tf_op | source)
XLA Modules:
  0.0 1937.2 jit_solution(6187918564265646572)
XLA Ops:
  7.2 1.4 copy.14
  8.5 29.3 %all-to-all-start = ((s32[32,1,8]{2,1,0:T(1,128)}), s32[32,1,8]{2,1,0:T(1,128)S(1)}, u32[]{:S(2)}, u32[]{:S(2)}) async-start(s32[32,1,8]{2,1,0:T(1,128)} %bitcast), calls=%async_computation | async-start | bytes 32768 | tf_op jit(solution)/shard_map/all_to_all | solution.py:65
  37.9 0.7 copy-done.3
  38.6 43.2 %scatter_custom_fusion.1 = f32[32768]{0:T(1024)S(1)} fusion(s32[8192]{0:T(1024)S(1)} %bitcast.88, f32[8192]{0:T(1024)S(1)} %broadcast.96, f32[]{:T(128)} %constant.15.clone.1), kind=kCustom, calls=%fused_computation.53 | custom fusion | flops 8192 | bytes 131076 | tf_op jit(solution)/shard_map/scatter-add | solution.py:53
  81.9 43.2 %scatter_custom_fusion = f32[32768]{0:T(1024)S(1)} fusion(s32[8192]{0:T(1024)S(1)} %bitcast.89, f32[8192]{0:T(1024)S(1)} %bitcast.93, f32[]{:T(128)} %constant.15.clone.1), kind=kCustom, calls=%fused_computation.55 | custom fusion | flops 8192 | bytes 131076 | tf_op jit(solution)/shard_map/scatter-add | solution.py:53
  125.2 0.9 maximum_bitcast_fusion
  126.1 21.2 %all-to-all-start.1 = ((f32[32,8,2,128]{3,2,1,0:T(2,128)}), f32[32,8,2,128]{3,2,1,0:T(2,128)S(1)}, u32[]{:S(2)}, u32[]{:S(2)}) async-start(f32[32,8,2,128]{3,2,1,0:T(2,128)} %maximum_bitcast_fusion), calls=%async_computation.1 | async-start | bytes 524288 | tf_op jit(solution)/shard_map/all_to_all | solution.py:64
  148.7 38.3 %all-to-all-done.1 = f32[32,8,2,128]{3,2,1,0:T(2,128)S(1)} async-done(((f32[32,8,2,128]{3,2,1,0:T(2,128)}), f32[32,8,2,128]{3,2,1,0:T(2,128)S(1)}, u32[]{:S(2)}, u32[]{:S(2)}) %all-to-all-start.1) | async-done | bytes 262176 | tf_op jit(solution)/shard_map/all_to_all | solution.py:64
  187.1 8.3 scatter_fusion
  196.3 157.7 %all-reduce.8.cloned.1.call-done = f32[256,2,128]{2,1,0:T(2,128)} async-done(((f32[256,2,128]{2,1,0:T(2,128)}), f32[256,2,128]{2,1,0:T(2,128)}) %all-reduce.8.cloned.1.call-update) | async-done | bytes 262160 | tf_op jit(solution)/shard_map/psum | solution.py:70
  354.0 1.3 slice_maximum_fusion
  355.2 1.3 gather_fusion
  356.6 22.6 %all-to-all-start.2 = ((f32[32,8,128]{2,1,0:T(8,128)}), f32[32,8,128]{2,1,0:T(8,128)S(1)}, u32[]{:S(2)}, u32[]{:S(2)}) async-start(f32[32,8,128]{2,1,0:T(8,128)} %bitcast.7), calls=%async_computation.2 | async-start | bytes 262144 | tf_op jit(solution)/shard_map/all_to_all | solution.py:74
  379.3 29.5 %all-to-all-done.2 = f32[32,8,128]{2,1,0:T(8,128)S(1)} async-done(((f32[32,8,128]{2,1,0:T(8,128)}), f32[32,8,128]{2,1,0:T(8,128)S(1)}, u32[]{:S(2)}, u32[]{:S(2)}) %all-to-all-start.2) | async-done | bytes 131104 | tf_op jit(solution)/shard_map/all_to_all | solution.py:74
  408.9 45.5 %gather_fusion.1 = f32[8192]{0:T(1024)S(1)} fusion(f32[32768]{0:T(1024)S(1)} %bitcast.68, s32[8192]{0:T(1024)S(1)} %broadcast_clamp_fusion), kind=kCustom, calls=%fused_computation.1 | custom fusion | bytes 98304 | tf_op jit(solution)/shard_map/gather | solution.py:75
  454.8 43.3 %scatter_custom_fusion.3 = f32[32768]{0:T(1024)S(1)} fusion(s32[8192]{0:T(1024)S(1)} %bitcast.90, f32[8192]{0:T(1024)S(1)} %reshape.232, f32[]{:T(128)} %constant.15.clone.1), kind=kCustom, calls=%fused_computation.51 | custom fusion | flops 8192 | bytes 131076 | tf_op jit(solution)/shard_map/scatter-add | solution.py:53
  498.0 30.8 %all_to_all.55 = f32[32,8,1,128]{3,1,2,0:T(8,128)S(1)} all-to-all(f32[32,8,1,128]{3,1,2,0:T(8,128)S(1)} %bitcast.80), channel_id=1, replica_groups=mesh['grp'=8,'blk'=32,'rep'=4] {'blk'}, dimensions={0} | all-to-all | bytes 262144 | tf_op jit(solution)/shard_map/all_to_all | solution.py:64
  528.8 2.0 scatter_custom_fusion.4
  530.9 157.2 %all-reduce.10.cloned.1.call-done = f32[256,1,128]{2,0,1:T(8,128)} async-done(((f32[256,1,128]{2,0,1:T(8,128)}), f32[256,1,128]{2,0,1:T(8,128)}) %all-reduce.10.cloned.1.call-update) | async-done | bytes 131088 | tf_op jit(solution)/shard_map/psum | solution.py:70
  688.1 0.9 divide_bitcast_fusion.1
  689.0 1.3 gather_fusion.2
  690.4 22.8 %all-to-all-start.4 = ((f32[32,8,128]{2,1,0:T(8,128)}), f32[32,8,128]{2,1,0:T(8,128)S(1)}, u32[]{:S(2)}, u32[]{:S(2)}) async-start(f32[32,8,128]{2,1,0:T(8,128)} %bitcast.15), calls=%async_computation.4 | async-start | bytes 262144 | tf_op jit(solution)/shard_map/all_to_all | solution.py:74
  713.8 29.0 %all-to-all-done.4 = f32[32,8,128]{2,1,0:T(8,128)S(1)} async-done(((f32[32,8,128]{2,1,0:T(8,128)}), f32[32,8,128]{2,1,0:T(8,128)S(1)}, u32[]{:S(2)}, u32[]{:S(2)}) %all-to-all-start.4) | async-done | bytes 131104 | tf_op jit(solution)/shard_map/all_to_all | solution.py:74
  742.8 45.5 %gather_fusion.3 = f32[8192]{0:T(1024)S(1)} fusion(f32[32768]{0:T(1024)S(1)} %bitcast.67, s32[8192]{0:T(1024)S(1)} %broadcast_clamp_fusion), kind=kCustom, calls=%fused_computation.3 | custom fusion | bytes 98304 | tf_op jit(solution)/shard_map/gather | solution.py:75
  788.6 0.8 multiply_reduce_fusion.4
  789.4 154.3 %all-reduce.2 = (f32[]{:T(128)}, f32[]{:T(128)}) all-reduce(f32[]{:T(128)} %get-tuple-element.7, f32[]{:T(128)} %get-tuple-element.6), channel_id=1, replica_groups=mesh['grp'=8,'blk'=32,'rep'=4] {'grp','blk','rep'}, use_global_device_ids=true, to_apply=%region_6.0 | all-reduce | flops 2 | bytes 16 | tf_op jit(solution)/shard_map/psum | solution.py:93
  945.1 43.3 %scatter_custom_fusion.5 = f32[32768]{0:T(1024)S(1)} fusion(s32[8192]{0:T(1024)S(1)} %bitcast.91, f32[8192]{0:T(1024)S(1)} %reshape.250, f32[]{:T(128)} %constant.15.clone.1), kind=kCustom, calls=%fused_computation.49 | custom fusion | flops 8192 | bytes 131076 | tf_op jit(solution)/shard_map/scatter-add | solution.py:53
  988.4 36.1 %all_to_all.56 = f32[32,8,1,128]{3,1,2,0:T(8,128)S(1)} all-to-all(f32[32,8,1,128]{3,1,2,0:T(8,128)S(1)} %bitcast.81), channel_id=1, replica_groups=mesh['grp'=8,'blk'=32,'rep'=4] {'blk'}, dimensions={0} | all-to-all | bytes 262144 | tf_op jit(solution)/shard_map/all_to_all | solution.py:64
  1024.5 2.0 scatter_custom_fusion.6
  1026.6 151.2 %all-reduce.12.cloned.1.call-done = f32[256,1,128]{2,0,1:T(8,128)} async-done(((f32[256,1,128]{2,0,1:T(8,128)}), f32[256,1,128]{2,0,1:T(8,128)}) %all-reduce.12.cloned.1.call-update) | async-done | bytes 131088 | tf_op jit(solution)/shard_map/psum | solution.py:70
  1177.8 0.9 divide_bitcast_fusion
  1178.7 1.3 gather_fusion.4
  1180.1 22.6 %all-to-all-start.6 = ((f32[32,8,128]{2,1,0:T(8,128)}), f32[32,8,128]{2,1,0:T(8,128)S(1)}, u32[]{:S(2)}, u32[]{:S(2)}) async-start(f32[32,8,128]{2,1,0:T(8,128)} %bitcast.22), calls=%async_computation.6 | async-start | bytes 262144 | tf_op jit(solution)/shard_map/all_to_all | solution.py:74
  1203.3 29.0 %all-to-all-done.6 = f32[32,8,128]{2,1,0:T(8,128)S(1)} async-done(((f32[32,8,128]{2,1,0:T(8,128)}), f32[32,8,128]{2,1,0:T(8,128)S(1)}, u32[]{:S(2)}, u32[]{:S(2)}) %all-to-all-start.6) | async-done | bytes 131104 | tf_op jit(solution)/shard_map/all_to_all | solution.py:74
  1232.3 45.5 %gather_fusion.5 = f32[8192]{0:T(1024)S(1)} fusion(f32[32768]{0:T(1024)S(1)} %bitcast.69, s32[8192]{0:T(1024)S(1)} %broadcast_clamp_fusion), kind=kCustom, calls=%fused_computation.5 | custom fusion | bytes 98304 | tf_op jit(solution)/shard_map/gather | solution.py:75
  1278.1 0.9 multiply_reduce_fusion.2
  1279.0 154.1 %all-reduce.1 = (f32[]{:T(128)}, f32[]{:T(128)}) all-reduce(f32[]{:T(128)} %get-tuple-element.5, f32[]{:T(128)} %get-tuple-element.4), channel_id=1, replica_groups=mesh['grp'=8,'blk'=32,'rep'=4] {'grp','blk','rep'}, use_global_device_ids=true, to_apply=%region_14.15 | all-reduce | flops 2 | bytes 16 | tf_op jit(solution)/shard_map/psum | solution.py:93
  1437.9 43.3 %scatter_custom_fusion.7 = f32[32768]{0:T(1024)S(1)} fusion(s32[8192]{0:T(1024)S(1)} %bitcast.92, f32[8192]{0:T(1024)S(1)} %reshape.268, f32[]{:T(128)} %constant.15.clone.1), kind=kCustom, calls=%fused_computation.47 | custom fusion | flops 8192 | bytes 131076 | tf_op jit(solution)/shard_map/scatter-add | solution.py:53
  1481.1 36.1 %all_to_all.57 = f32[32,8,1,128]{3,1,2,0:T(8,128)S(1)} all-to-all(f32[32,8,1,128]{3,1,2,0:T(8,128)S(1)} %bitcast.79), channel_id=1, replica_groups=mesh['grp'=8,'blk'=32,'rep'=4] {'blk'}, dimensions={0} | all-to-all | bytes 262144 | tf_op jit(solution)/shard_map/all_to_all | solution.py:64
  1517.3 2.0 scatter_custom_fusion.8
  1519.3 151.3 %all-reduce.14.cloned.1.call-done = f32[256,1,128]{2,1,0:T(1,128)} async-done(((f32[256,1,128]{2,1,0:T(1,128)}), f32[256,1,128]{2,1,0:T(1,128)}) %all-reduce.14.cloned.1.call-update) | async-done | bytes 131088 | tf_op jit(solution)/shard_map/psum | solution.py:70
  1670.7 1.1 fusion.108
  1671.8 1.3 gather_fusion.6
  1673.1 22.6 %all-to-all-start.8 = ((f32[32,8,128]{2,1,0:T(8,128)}), f32[32,8,128]{2,1,0:T(8,128)S(1)}, u32[]{:S(2)}, u32[]{:S(2)}) async-start(f32[32,8,128]{2,1,0:T(8,128)} %bitcast.28), calls=%async_computation.8 | async-start | bytes 262144 | tf_op jit(solution)/shard_map/all_to_all | solution.py:74
  1696.3 29.1 %all-to-all-done.8 = f32[32,8,128]{2,1,0:T(8,128)S(1)} async-done(((f32[32,8,128]{2,1,0:T(8,128)}), f32[32,8,128]{2,1,0:T(8,128)S(1)}, u32[]{:S(2)}, u32[]{:S(2)}) %all-to-all-start.8) | async-done | bytes 131104 | tf_op jit(solution)/shard_map/all_to_all | solution.py:74
  1725.4 45.5 %gather_fusion.7 = f32[8192]{0:T(1024)S(1)} fusion(f32[32768]{0:T(1024)S(1)} %bitcast.70, s32[8192]{0:T(1024)S(1)} %broadcast_clamp_fusion), kind=kCustom, calls=%fused_computation.7 | custom fusion | bytes 98304 | tf_op jit(solution)/shard_map/gather | solution.py:75
  1771.1 0.8 multiply_reduce_fusion
  1771.9 154.1 %all-reduce = (f32[]{:T(128)}, f32[]{:T(128)}) all-reduce(f32[]{:T(128)} %get-tuple-element.3, f32[]{:T(128)} %get-tuple-element.2), channel_id=1, replica_groups=mesh['grp'=8,'blk'=32,'rep'=4] {'grp','blk','rep'}, use_global_device_ids=true, to_apply=%region_22.23 | all-reduce | flops 2 | bytes 16 | tf_op jit(solution)/shard_map/psum | solution.py:93
  (63 shorter events, 6.2 us)
Async XLA Ops:
  7.2 30.7 %copy-start.2 = (f32[8,1024]{1,0:T(8,128)S(1)}, f32[8,1024]{1,0:T(8,128)}, u32[]{:S(2)}) copy-start(f32[8,1024]{1,0:T(8,128)} %param.5) | copy-start | bytes 98308
  8.5 117.6 %all-to-all-start = ((s32[32,1,8]{2,1,0:T(1,128)}), s32[32,1,8]{2,1,0:T(1,128)S(1)}, u32[]{:S(2)}, u32[]{:S(2)}) async-start(s32[32,1,8]{2,1,0:T(1,128)} %bitcast), calls=%async_computation | async-start | bytes 32768 | tf_op jit(solution)/shard_map/all_to_all | solution.py:65
  37.8 0.8 copy-start.3
  37.8 0.8 copy-start.4
  126.1 60.9 %all-to-all-start.1 = ((f32[32,8,2,128]{3,2,1,0:T(2,128)}), f32[32,8,2,128]{3,2,1,0:T(2,128)S(1)}, u32[]{:S(2)}, u32[]{:S(2)}) async-start(f32[32,8,2,128]{3,2,1,0:T(2,128)} %maximum_bitcast_fusion), calls=%async_computation.1 | async-start | bytes 524288 | tf_op jit(solution)/shard_map/all_to_all | solution.py:64
  147.3 206.6 %all-reduce.8.cloned.1.call-start = ((), (), s32[]{:S(2)}) async-start(), calls=%async_computation.9 | async-start | bytes 524288 | tf_op jit(solution)/shard_map/psum | solution.py:70
  195.5 0.7 copy-start
  356.6 52.3 %all-to-all-start.2 = ((f32[32,8,128]{2,1,0:T(8,128)}), f32[32,8,128]{2,1,0:T(8,128)S(1)}, u32[]{:S(2)}, u32[]{:S(2)}) async-start(f32[32,8,128]{2,1,0:T(8,128)} %bitcast.7), calls=%async_computation.2 | async-start | bytes 262144 | tf_op jit(solution)/shard_map/all_to_all | solution.py:74
  379.2 308.9 %all-reduce.10.cloned.1.call-start = ((), (), s32[]{:S(2)}) async-start(), calls=%async_computation.10 | async-start | bytes 262144 | tf_op jit(solution)/shard_map/psum | solution.py:70
  690.4 22.8 %copy-start.5 = (f32[8,9]{1,0:T(8,128)S(1)}, f32[8,9]{1,0:T(8,128)}, u32[]{:S(2)}) copy-start(f32[8,9]{1,0:T(8,128)} %param.9) | copy-start | bytes 868
  690.4 52.4 %all-to-all-start.4 = ((f32[32,8,128]{2,1,0:T(8,128)}), f32[32,8,128]{2,1,0:T(8,128)S(1)}, u32[]{:S(2)}, u32[]{:S(2)}) async-start(f32[32,8,128]{2,1,0:T(8,128)} %bitcast.15), calls=%async_computation.4 | async-start | bytes 262144 | tf_op jit(solution)/shard_map/all_to_all | solution.py:74
  713.2 464.6 %all-reduce.12.cloned.1.call-start = ((), (), s32[]{:S(2)}) async-start(), calls=%async_computation.11 | async-start | bytes 262144 | tf_op jit(solution)/shard_map/psum | solution.py:70
  1180.1 52.3 %all-to-all-start.6 = ((f32[32,8,128]{2,1,0:T(8,128)}), f32[32,8,128]{2,1,0:T(8,128)S(1)}, u32[]{:S(2)}, u32[]{:S(2)}) async-start(f32[32,8,128]{2,1,0:T(8,128)} %bitcast.22), calls=%async_computation.6 | async-start | bytes 262144 | tf_op jit(solution)/shard_map/all_to_all | solution.py:74
  1202.7 467.9 %all-reduce.14.cloned.1.call-start = ((), (), s32[]{:S(2)}) async-start(), calls=%async_computation.12 | async-start | bytes 262144 | tf_op jit(solution)/shard_map/psum | solution.py:70
  1517.3 153.4 %copy-start.1 = (f32[256,2,128]{2,1,0:T(2,128)S(1)}, f32[256,2,128]{2,1,0:T(2,128)}, u32[]{:S(2)}) copy-start(f32[256,2,128]{2,1,0:T(2,128)} %all-reduce.8.cloned.1.call-done) | copy-start | bytes 786436
  1673.1 52.3 %all-to-all-start.8 = ((f32[32,8,128]{2,1,0:T(8,128)}), f32[32,8,128]{2,1,0:T(8,128)S(1)}, u32[]{:S(2)}, u32[]{:S(2)}) async-start(f32[32,8,128]{2,1,0:T(8,128)} %bitcast.28), calls=%async_computation.8 | async-start | bytes 262144 | tf_op jit(solution)/shard_map/all_to_all | solution.py:74
Sparse Core Ops, SparseCore 0:
  196.3 157.6 all-reduce.7
  531.0 157.0 all-reduce.9
  1026.7 151.0 all-reduce.11
  1519.4 151.1 all-reduce.13
where the time goes:
time: 1940 us
  waiting for transfers between devices  772 us (40%)
  blocking collectives  566 us (29%)
  other arithmetic  238 us (12%)
  local copies, waits for them, and re-layouts  192 us (10%)
  starting transfers between devices  141 us (7%)
  between operations  24.1 us (1%)
    psum x4, waiting for transfers between devices, project(): return (lax.psum(segment, ('grp', 'rep')), received_ids)  617 us
    psum x3, blocking collectives, pairwise_inner(): lax.psum((jnp.sum(leftover_error * leftover_error), jnp.sum(leftover_erro...  463 us
    scatter-add x5, other arithmetic, bin_one(): jax.ops.segment_sum(flat_field, local_index, num_segments=owners * per_ow...  216 us
    gather x4, local copies, waits for them, and re-layouts, read_back(): return returned.reshape(-1)[local_index].reshape(detectors, samples)  182 us
    all_to_all x4, waiting for transfers between devices, read_back(): lax.all_to_all(wanted, 'blk', split_axis=0, concat_axis=0, tiled=True)  117 us
    all_to_all x3, blocking collectives, project(): lax.all_to_all(partial_value, 'blk', split_axis=0, concat_axis=0, tiled=T...  103 us
    all_to_all x4, starting transfers between devices, read_back(): lax.all_to_all(wanted, 'blk', split_axis=0, concat_axis=0, tiled=True)  90.7 us
  transfers between devices with their start and end apart: 10, of which 9 were waited for; matrix products, arithmetic and copies ran while one was open for 5% of the time, Pallas kernels for 0%

commit v1 on v0

v1 whole, which is shorter than its diff:
```python
import functools
import math

import jax
import jax.numpy as jnp
from jax import lax
from jax.experimental import pallas as pl
from jax.experimental.pallas import tpu as pltpu
from jax.sharding import PartitionSpec as P

BL = 64
K = 8
LISTS_HERE = 8
REPS = 4
PLANE = 32
LINE = 32
SHARE = 4
DET = 8
SAMP = 1024
LANES = 128
BASES = 16
TILES = SAMP // LANES
ITERS = 3
F32 = jnp.float32
BF16 = jnp.bfloat16
MESH = pl.DeviceIdType.MESH

IDS, TOD, HITS, FIRST = 0, 1, 2, 3
OUT = 6
BACK = 4


def pieces(value, count):
    parts = []
    for _ in range(count):
        part = value.astype(BF16)
        value = value - part.astype(F32)
        parts.append(part)
    return parts


def lanes_of(shape):
    return lax.broadcasted_iota(jnp.int32, shape, len(shape) - 1)


def kernel(
    ids_ref, tod_ref, slot_ref, off_ref, prior_ref, x_ref, r_ref,
    s_hot, o_hot, id_hot, acc, part, tmp, mt, yrow, tot,
    psend, prec, zsend, zrec, bsend, brec, csend, crec, ssend, srec, tsend, trec,
    ps_sem, pr_sem, zs_sem, zr_sem, bs_sem, br_sem, cs_sem, cr_sem,
    ss_sem, sr_sem, ts_sem, tr_sem,
):
    grp = lax.axis_index("grp")
    blk = lax.axis_index("blk")
    rep = lax.axis_index("rep")
    me = grp * REPS + rep
    chips = LISTS_HERE // 2

    def plane_peer(i):
        dx, dc, dy = i // (2 * REPS), (i // REPS) % 2, i % REPS
        g = ((grp // 2 + dx) % chips) * 2 + (grp % 2 + dc) % 2
        return g, (rep + dy) % REPS

    def line_peer(i):
        return (blk + LINE // 2 + (1 - 2 * (i % 2)) * ((i + 1) // 2)) % LINE

    def plane_send(source, target, send, recv):
        @pl.loop(1, PLANE)
        def _(i):
            g, y = plane_peer(i)
            pltpu.make_async_remote_copy(
                src_ref=source(g, y), dst_ref=target, send_sem=send, recv_sem=recv,
                device_id={"grp": g, "rep": y}, device_id_type=MESH,
            ).start()

    def line_send(source, target, send, recv):
        @pl.loop(0, LINE - 1)
        def _(i):
            z = line_peer(i)
            pltpu.make_async_remote_copy(
                src_ref=source(z), dst_ref=target, send_sem=send, recv_sem=recv,
                device_id={"blk": z}, device_id_type=MESH,
            ).start()

    def arrived(view, sem):
        pltpu.make_async_copy(view, view, sem).wait()

    barrier = pltpu.get_barrier_semaphore()

    @pl.loop(1, PLANE)
    def _(i):
        g, y = plane_peer(i)
        pl.semaphore_signal(barrier, inc=1, device_id={"grp": g, "rep": y}, device_id_type=MESH)

    @pl.loop(0, LINE - 1)
    def _(i):
        pl.semaphore_signal(
            barrier, inc=1, device_id={"blk": line_peer(i)}, device_id_type=MESH
        )

    pl.semaphore_wait(barrier, PLANE + LINE - 2)

    for kh in range(2):
        tile = jnp.broadcast_to(ids_ref[kh : kh + 1, :], (SHARE, LANES))
        psend[IDS, 0, kh * SHARE : (kh + 1) * SHARE, :] = tile
        prec[IDS, me, kh * SHARE : (kh + 1) * SHARE, :] = tile
    plane_send(
        lambda g, y: psend.at[IDS, 0], prec.at[IDS, me], ps_sem.at[IDS], pr_sem.at[IDS]
    )

    @pl.loop(0, DET)
    def _(d):
        slot = slot_ref[pl.ds(d, 1), :]
        place = (slot % K) * LINE + slot // K
        rows = lax.broadcasted_iota(jnp.int32, (LINE * K, SAMP), 0)
        s_hot[d] = jnp.where(rows == place, 1.0, 0.0).astype(BF16)
        rows = lax.broadcasted_iota(jnp.int32, (LANES, SAMP), 0)
        o_hot[d] = jnp.where(rows == off_ref[pl.ds(d, 1), :], 1.0, 0.0).astype(BF16)

    def local_map(first):
        acc[...] = jnp.zeros_like(acc)

        @pl.loop(0, DET)
        def _(d):
            hot = o_hot[d]
            left = []
            for p in (first, first + 1):
                row = part[p, pl.ds(d, 1), :]
                left.append(hot * jnp.broadcast_to(row, (LANES, SAMP)).astype(BF16))
            acc[...] += lax.dot_general(
                jnp.concatenate(left, axis=0), s_hot[d],
                (((1,), (1,)), ((), ())), preferred_element_type=F32,
            )

    def send_map(f, image):
        for g in range(PLANE):
            for kh in range(2):
                psend[f, g, kh * SHARE : (kh + 1) * SHARE, :] = image[
                    g * SHARE : (g + 1) * SHARE, kh * LANES : (kh + 1) * LANES
                ]
        prec[f, me] = psend[f, me]
        plane_send(
            lambda g, y: psend.at[f, g * REPS + y], prec.at[f, me], ps_sem.at[f], pr_sem.at[f]
        )

    def to_owners(f):
        arrived(prec.at[f, pl.ds(0, PLANE - 1)], pr_sem.at[f])
        for l in range(LISTS_HERE):
            total = prec[f, l * REPS]
            for y in range(1, REPS):
                total = total + prec[f, l * REPS + y]
            tmp[l * 8 : l * 8 + 8, :] = total
        half = [
            [tmp[pl.ds(kh * SHARE + j, 8, stride=8), :] for kh in range(2)] for j in range(SHARE)
        ]
        lane = lanes_of((8, LANES))
        groups = []
        for kqh in range(2):
            for j in range(SHARE):
                for kql in range(2):
                    kq = kqh * 2 + kql
                    low = pltpu.roll(half[j][0], (-32 * kq) % LANES, 1)
                    high = pltpu.roll(half[j][1], (32 - 32 * kq) % LANES, 1)
                    groups.append(jnp.where(lane < 32, low, high))
        turned = jnp.transpose(jnp.concatenate(groups, axis=0))
        for kh in range(2):
            zsend[f, kh] = turned[kh * LINE : (kh + 1) * LINE].reshape(LINE, 1, LANES)
        zrec[f, :, blk] = zsend[f, :, blk]
        line_send(
            lambda z: zsend.at[f, :, z], zrec.at[f, :, blk], zs_sem.at[f], zr_sem.at[f]
        )

    def at_owner(f):
        arrived(zrec.at[f, :, pl.ds(0, LINE - 1)], zr_sem.at[f])
        rows = jnp.concatenate(
            [zrec[f, kh].reshape(LINE, LANES) for kh in range(2)], axis=0
        )
        both = jnp.concatenate([rows, pltpu.roll(rows, 64, 1)], axis=0)
        tmp[...] = jnp.transpose(both)[:64]
        return jnp.concatenate(
            [tmp[pl.ds(b, SHARE, stride=16), :] for b in range(16)], axis=1
        )

    def merged(f):
        left = jnp.concatenate(pieces(at_owner(f), 3), axis=0)
        out = lax.dot_general(
            left, id_hot[...], (((1,), (1,)), ((), ())), preferred_element_type=F32
        )
        return out[:SHARE] + out[SHARE : 2 * SHARE] + out[2 * SHARE :]

    def send_back(b, values):
        left = jnp.concatenate(pieces(values, 3), axis=0)
        out = jnp.dot(left, id_hot[...], preferred_element_type=F32)
        out = out[:SHARE] + out[SHARE : 2 * SHARE] + out[2 * SHARE :]
        for c in range(16):
            tmp[pl.ds(c, SHARE, stride=16), :] = out[:, c * LANES : (c + 1) * LANES]
        turned = jnp.transpose(
            jnp.concatenate([tmp[...], jnp.zeros((64, LANES), F32)], axis=0)
        )
        rows = jnp.where(
            lanes_of((64, LANES)) < 64, turned[:64], pltpu.roll(turned[64:], 64, 1)
        )
        for kh in range(2):
            bsend[b, kh] = rows[kh * LINE : (kh + 1) * LINE].reshape(LINE, 1, LANES)
        brec[b, :, blk] = bsend[b, :, blk]
        line_send(
            lambda z: bsend.at[b, :, z], brec.at[b, :, blk], bs_sem.at[b], br_sem.at[b]
        )

    def to_lists(b):
        arrived(brec.at[b, :, pl.ds(0, LINE - 1)], br_sem.at[b])
        rows = jnp.concatenate(
            [brec[b, kh].reshape(LINE, LANES) for kh in range(2)], axis=0
        )
        turned = jnp.transpose(
            jnp.concatenate([rows, jnp.zeros((64, LANES), F32)], axis=0)
        )
        quarter = lanes_of((8, LANES)) // 32
        for j in range(SHARE):
            for kh in range(2):
                tile = jnp.zeros((8, LANES), F32)
                for kq in range(4):
                    start = (kq // 2) * 64 + j * 16 + (kq % 2) * 8
                    moved = pltpu.roll(
                        turned[start : start + 8], (32 * kq - 32 * kh) % LANES, 1
                    )
                    tile = jnp.where(quarter == kq, moved, tile)
                csend[b, pl.ds(kh * SHARE + j, 8, stride=8), :] = tile
        crec[b, me] = csend[b, pl.ds(pl.multiple_of(grp * 8, 8), 8), :]
        plane_send(
            lambda g, y: csend.at[b, pl.ds(pl.multiple_of(g * 8, 8), 8)],
            crec.at[b, me], cs_sem.at[b], cr_sem.at[b],
        )

    def picked(b, count):
        arrived(crec.at[b, pl.ds(0, PLANE - 1)], cr_sem.at[b])
        for kh in range(2):
            for g in range(0, PLANE, 2):
                at = slice(kh * SHARE, (kh + 1) * SHARE)
                rows = jnp.concatenate([crec[b, g, at, :], crec[b, g + 1, at, :]], axis=0)
                acc[g * SHARE : g * SHARE + 8, kh * LANES : (kh + 1) * LANES] = rows
        for p, piece in enumerate(pieces(acc[:LANES, :], count)):
            mt[p * LANES : (p + 1) * LANES, :] = piece

        @pl.loop(0, DET)
        def _(d):
            out = jnp.dot(mt[: count * LANES, :], s_hot[d], preferred_element_type=F32)
            total = out[:LANES]
            for p in range(1, count):
                total = total + out[p * LANES : (p + 1) * LANES]
            yrow[pl.ds(d, 1), :] = jnp.sum(
                total * o_hot[d].astype(F32), axis=0, keepdims=True
            )

        return folded(yrow[...])

    def tiles(value):
        return [value[:, t * LANES : (t + 1) * LANES] for t in range(TILES)]

    def folded(value):
        stacked = jnp.concatenate(tiles(value), axis=0)
        a = lax.broadcasted_iota(jnp.int32, (LANES, LANES), 0) // BL
        b = lanes_of((LANES, LANES)) // BL
        ones = jnp.where(a == b, 1.0, 0.0).astype(BF16)
        left = jnp.concatenate(pieces(stacked, 3), axis=0)
        out = jnp.dot(left, ones, preferred_element_type=F32)
        out = out[:64] + out[64:128] + out[128:]
        return jnp.concatenate([out[t * 8 : t * 8 + 8] for t in range(TILES)], axis=1)

    def smoothed(value):
        here = tiles(value)
        swapped = [pltpu.roll(t, 64, 1) for t in here]
        low = lanes_of((DET, LANES)) < 64
        odd = [jnp.where(low, swapped[t - 1], swapped[t]) for t in range(TILES)]
        spectrum = [
            jnp.broadcast_to(prior_ref[:, f : f + 1], (DET, LANES)) for f in range(BASES // 2 + 1)
        ]
        out = [jnp.zeros((DET, LANES), F32) for _ in range(TILES)]
        for shift in range(BASES):
            weight = jnp.zeros((DET, LANES), F32)
            for f in range(BASES // 2 + 1):
                share = (1.0 if f in (0, BASES // 2) else 2.0) / BASES
                weight = weight + spectrum[f] * (
                    share * math.cos(2.0 * math.pi * ((f * shift) % BASES) / BASES)
                )
            source = odd if shift % 2 else here
            for t in range(TILES):
                out[t] = out[t] + weight * source[(t - shift // 2) % TILES]
        return jnp.concatenate(out, axis=1)

    def lane_sums(value):
        total = functools.reduce(lambda a, b: a + b, tiles(value))
        total = jnp.sum(total, axis=0, keepdims=True)
        return total + pltpu.roll(total, 64, 1)

    for p, piece in enumerate(pieces(tod_ref[...], 3)):
        part[p] = piece.astype(F32)
    part[3] = jnp.ones((DET, SAMP), F32)
    local_map(0)
    held = acc[:LANES, :] + acc[LANES:, :]
    local_map(2)
    send_map(TOD, held + acc[:LANES, :])
    send_map(HITS, acc[LANES:, :])
    to_owners(IDS)
    to_owners(TOD)
    to_owners(HITS)
    ids = at_owner(IDS)[0:1, :].astype(jnp.int32)
    rows = lax.broadcasted_iota(jnp.int32, (256, LINE * LISTS_HERE * K), 0)
    id_hot[...] = jnp.where(rows == ids, 1.0, 0.0).astype(BF16)
    sums = merged(TOD)
    divisor = jnp.maximum(merged(HITS), 1.0)
    send_back(0, sums / divisor)
    source = folded(tod_ref[...])
    to_lists(0)
    residual = source - picked(0, 3)

    def apply(n, value):
        f, b = FIRST + n, 1 + n
        for p, piece in enumerate(pieces(value, 2)):
            part[p] = piece.astype(F32)
        local_map(0)
        send_map(f, acc[:LANES, :] + acc[LANES:, :])
        rest = BL * value + smoothed(value)
        square = lane_sums(value * value) * (1.0 / BL)
        product = lane_sums(value * rest) * (1.0 / BL)
        to_owners(f)
        sums = merged(f)
        binned = sums / divisor
        energy = jnp.sum(sums * binned, axis=0, keepdims=True)
        energy = energy[:, :LANES] + energy[:, LANES:]
        energy = energy + pltpu.roll(energy, 64, 1)
        low = lanes_of((1, LANES)) < 64
        row = jnp.where(low, square, product - energy)
        ssend[n] = row
        srec[n, blk] = row
        line_send(lambda z: ssend.at[n], srec.at[n, blk], ss_sem.at[n], sr_sem.at[n])
        send_back(b, binned)
        arrived(srec.at[n, pl.ds(0, LINE - 1)], sr_sem.at[n])
        row = jnp.sum(srec[n], axis=0)
        tsend[n] = row
        trec[n, me] = row
        plane_send(lambda g, y: tsend.at[n], trec.at[n, me], ts_sem.at[n], tr_sem.at[n])
        to_lists(b)
        image = rest - picked(b, 2)
        arrived(trec.at[n, pl.ds(0, PLANE - 1)], tr_sem.at[n])
        row = jnp.sum(trec[n], axis=0)
        rr = jnp.sum(jnp.where(low, row, 0.0), axis=1, keepdims=True)
        curve = jnp.sum(jnp.where(low, 0.0, row), axis=1, keepdims=True)
        return image, rr, curve

    iterate = jnp.zeros((DET, SAMP), F32)
    image, rr, curve = apply(0, residual)
    step = rr / curve
    direction, along = residual, image
    for it in range(ITERS):
        iterate = iterate + step * direction
        residual = residual - step * along
        if it + 1 < ITERS:
            image, new, curve = apply(it + 1, residual)
            ratio = new / rr
            step = new / (curve - ratio * new / step)
            direction = residual + ratio * direction
            along = image + ratio * along
            rr = new

    for ref, value in ((x_ref, iterate), (r_ref, residual)):
        out = jnp.zeros((DET, LANES), F32)
        lane = lanes_of((DET, LANES))
        for t, tile in enumerate(tiles(value)):
            for side in range(2):
                spread = jnp.broadcast_to(tile[:, side * BL : side * BL + 1], (DET, LANES))
                out = jnp.where(lane == 2 * t + side, spread, out)
        ref[...] = out[:, :BASES]

    for f in range(OUT):
        arrived(prec.at[f, pl.ds(0, PLANE - 1)], ps_sem.at[f])
        arrived(zrec.at[f, :, pl.ds(0, LINE - 1)], zs_sem.at[f])
    for b in range(BACK):
        arrived(brec.at[b, :, pl.ds(0, LINE - 1)], bs_sem.at[b])
        arrived(crec.at[b, pl.ds(0, PLANE - 1)], cs_sem.at[b])
    for n in range(ITERS):
        arrived(srec.at[n, pl.ds(0, LINE - 1)], ss_sem.at[n])
        arrived(trec.at[n, pl.ds(0, PLANE - 1)], ts_sem.at[n])


def shards(tod, hit_ids, sample_slot, sample_offset, prior):
    ids = hit_ids[0].T.reshape(2, LANES).astype(F32) * 0.25
    whole = pl.BlockSpec(memory_space=pltpu.VMEM)
    dma = pltpu.SemaphoreType.DMA
    return pl.pallas_call(
        kernel,
        out_shape=[jax.ShapeDtypeStruct((DET, BASES), F32)] * 2,
        in_specs=[whole] * 5,
        out_specs=[whole] * 2,
        scratch_shapes=[
            pltpu.VMEM((DET, LINE * K, SAMP), BF16),
            pltpu.VMEM((DET, LANES, SAMP), BF16),
            pltpu.VMEM((256, LINE * LISTS_HERE * K), BF16),
            pltpu.VMEM((256, 256), F32),
            pltpu.VMEM((4, DET, SAMP), F32),
            pltpu.VMEM((64, LANES), F32),
            pltpu.VMEM((3 * LANES, 256), BF16),
            pltpu.VMEM((DET, SAMP), F32),
            pltpu.VMEM((DET, SAMP), F32),
            pltpu.VMEM((OUT, PLANE, 8, LANES), F32),
            pltpu.VMEM((OUT, PLANE, 8, LANES), F32),
            pltpu.VMEM((OUT, 2, LINE, 1, LANES), F32),
            pltpu.VMEM((OUT, 2, LINE, 1, LANES), F32),
            pltpu.VMEM((BACK, 2, LINE, 1, LANES), F32),
            pltpu.VMEM((BACK, 2, LINE, 1, LANES), F32),
            pltpu.VMEM((BACK, 64, LANES), F32),
            pltpu.VMEM((BACK, PLANE, 8, LANES), F32),
            pltpu.VMEM((ITERS, 1, LANES), F32),
            pltpu.VMEM((ITERS, LINE, 1, LANES), F32),
            pltpu.VMEM((ITERS, 1, LANES), F32),
            pltpu.VMEM((ITERS, PLANE, 1, LANES), F32),
        ]
        + [dma((OUT,))] * 4 + [dma((BACK,))] * 4 + [dma((ITERS,))] * 4,
        compiler_params=pltpu.CompilerParams(
            collective_id=0, has_side_effects=True, vmem_limit_bytes=40 * 1024 * 1024
        ),
    )(ids, tod, sample_slot, sample_offset, prior)


def solution(mesh):
    rows = P(("grp", "blk", "rep"), None)
    return jax.shard_map(
        shards,
        mesh=mesh,
        in_specs=(rows, P(("grp", "blk"), None, None), rows, rows, rows),
        out_specs=(rows, rows),
        check_vma=False,
    )
```

time: 1940 us -> 215 us (0.11)
  waiting for transfers between devices: 772 us -> 0 us
  blocking collectives: 566 us -> 0 us
  other arithmetic: 238 us -> 0.69 us
  Pallas kernels: 0 us -> 209 us
  local copies, waits for them, and re-layouts: 192 us -> 4.15 us
  starting transfers between devices: 141 us -> 0 us
  between operations: 24.1 us -> 0.64 us
    psum x4 -> x0, waiting for transfers between devices: 617 us -> none  [project(): return (lax.psum(segment, ('grp', 'rep')), received_ids)]
    psum x3 -> x0, blocking collectives: 463 us -> none  [pairwise_inner(): lax.psum((jnp.sum(leftover_error * leftover_error), jnp.sum(leftover_erro...]
    scatter-add x9 -> x0, other arithmetic: 231 us -> none  [the longest x5 216 us: bin_one(): jax.ops.segment_sum(flat_field, local_index, num_segments=owners * per_ow...]
    pallas_call x0 -> x1, Pallas kernels: none -> 209 us  [shards(): pl.pallas_call(kernel, out_shape=[jax.ShapeDtypeStruct((DET, BASES), F32)...]
    gather x8 -> x0, local copies, waits for them, and re-layouts: 187 us -> none  [the longest x4 182 us: read_back(): return returned.reshape(-1)[local_index].reshape(detectors, samples)]
    all_to_all x6 -> x0, waiting for transfers between devices: 155 us -> none  [the longest x4 117 us: read_back(): lax.all_to_all(wanted, 'blk', split_axis=0, concat_axis=0, tiled=True)]
    all_to_all x6 -> x0, starting transfers between devices: 141 us -> none  [the longest x4 90.7 us: read_back(): lax.all_to_all(wanted, 'blk', split_axis=0, concat_axis=0, tiled=True)]
    all_to_all x3 -> x0, blocking collectives: 103 us -> none  [project(): lax.all_to_all(partial_value, 'blk', split_axis=0, concat_axis=0, tiled=T...]
  transfers between devices with their start and end apart: 10 -> 0, of which waited for: 9 -> 0; matrix products, arithmetic and copies ran while one was open for 5% -> 0% of each run, Pallas kernels for 0% -> 0%
where the time goes in v1:
time: 215 us
  Pallas kernels  209 us (97%)
  local copies, waits for them, and re-layouts  4.15 us (2%)
    pallas_call x1, Pallas kernels, shards(): pl.pallas_call(kernel, out_shape=[jax.ShapeDtypeStruct((DET, BASES), F32)...  209 us

profile of v1, /device:TPU:1, one launch (start us, length us, event | category | flops | bytes accessed | tf_op | source)
XLA Modules:
  0.0 214.8 jit_solution(59545026843911732)
XLA Ops:
  0.6 0.7 multiply_bitcast_fusion
  1.3 0.0 copy-start.3
  1.3 0.1 mul.16.ids_ref
  1.4 0.6 copy-done.3
  2.0 0.0 copy-start
  2.0 0.8 copy-done
  2.8 0.0 copy-start.1
  2.8 0.8 copy-done.1
  3.5 0.0 copy-start.2
  3.5 0.8 copy-done.2
  4.3 209.3 %shard_map.68 = (f32[8,16]{1,0:T(8,128)S(1)}, f32[8,16]{1,0:T(8,128)S(1)}) custom-call(f32[2,128]{1,0:T(2,128)S(1)} %mul.16.ids_ref, f32[8,1024]{1,0:T(8,128)S(1)} %copy-done, s32[8,1024]{1,0:T(8,128)S(1)} %copy-done.1, s32[8,1024]{1,0:T(8,128)S(1)} %copy-done.2, f32[8,9]{1,0:T(8,128)S(1)} %copy-done.3), custom_call_target="tpu_custom_call" | custom-call | tf_op jit(solution)/shard_map/pallas_call | solution.py:390
  213.6 0.6 copy.9
  214.2 0.6 copy.10
Async XLA Ops:
  1.3 0.7 copy-start.3
  2.0 0.8 copy-start
  2.8 0.8 copy-start.1
  3.5 0.8 copy-start.2

commit v2 on v1

v2 whole, which is shorter than its diff:
```python
import functools
import math

import jax
import jax.numpy as jnp
from jax import lax
from jax.experimental import pallas as pl
from jax.experimental.pallas import tpu as pltpu
from jax.sharding import PartitionSpec as P

BL = 64
K = 8
LISTS_HERE = 8
REPS = 4
PLANE = 32
LINE = 32
SHARE = 4
DET = 8
SAMP = 1024
LANES = 128
BASES = 16
TILES = SAMP // LANES
ITERS = 3
COPIES = 2
WINDOW = LINE // COPIES
ROWS = 2 * COPIES
F32 = jnp.float32
BF16 = jnp.bfloat16
MESH = pl.DeviceIdType.MESH

ROUNDS = 1 + ITERS
HITS = ROUNDS
OUT = ROUNDS + 1


def pieces(value, count):
    parts = []
    for _ in range(count):
        part = value.astype(BF16)
        value = value - part.astype(F32)
        parts.append(part)
    return parts


def lanes_of(shape):
    return lax.broadcasted_iota(jnp.int32, shape, len(shape) - 1)


def kernel(
    ids_in, tod_in, slot_in, off_in, prior_in, x_ref, r_ref,
    ids_ref, tod_ref, slot_ref, off_ref, prior_ref, in_sem,
    idsend, idz, idq, idp, id_sem, iterate, residual, direction, along, rest, held, divisor, rr_ref, step_ref,
    s_hot, o_hot, id_hot, near_hot, acc, part, tmp, mt, yrow,
    psend, prec, zsend, zrec, bsend, brec, csend, crec, ssend, srec, tsend, trec, wsend, wrec, usend, urec,
    ps_sem, pr_sem, zs_sem, zr_sem, bs_sem, br_sem, cs_sem, cr_sem,
    ss_sem, sr_sem, ts_sem, tr_sem, ws_sem, wr_sem, us_sem, ur_sem,
):
    grp = lax.axis_index("grp")
    blk = lax.axis_index("blk")
    rep = lax.axis_index("rep")
    me = grp * REPS + rep
    chips = LISTS_HERE // 2

    def farthest_first(i, size):
        return size // 2 + (1 - 2 * (i % 2)) * ((i + 1) // 2)

    def plane_peer(i):
        dx, dc, dy = i // (2 * REPS), (i // REPS) % 2, i % REPS
        g = ((grp // 2 + dx) % chips) * 2 + (grp % 2 + dc) % 2
        return g, (rep + dy) % REPS

    def line_peer(i):
        return (blk + farthest_first(i, LINE)) % LINE

    def near_step(i):
        step = (WINDOW // 2 - (i + 1) // 2) * (2 * (i % 2) - 1)
        return step

    def plane_send(source, target, send, recv):
        @pl.loop(1, PLANE)
        def _(i):
            g, y = plane_peer(i)
            pltpu.make_async_remote_copy(
                src_ref=source(g, y), dst_ref=target, send_sem=send, recv_sem=recv,
                device_id={"grp": g, "rep": y}, device_id_type=MESH,
            ).start()

    def line_send(source, target, send, recv):
        @pl.loop(0, LINE - 1)
        def _(i):
            z = line_peer(i)
            pltpu.make_async_remote_copy(
                src_ref=source(z), dst_ref=target(z), send_sem=send, recv_sem=recv,
                device_id={"blk": z}, device_id_type=MESH,
            ).start()

    def near_send(source, target, send, recv):
        @pl.loop(0, WINDOW - 1)
        def _(i):
            step = near_step(i)
            pltpu.make_async_remote_copy(
                src_ref=source(step), dst_ref=target, send_sem=send, recv_sem=recv,
                device_id={"blk": (blk + step + LINE) % LINE}, device_id_type=MESH,
            ).start()

    def arrived(view, sem):
        pltpu.make_async_copy(view, view, sem).wait()

    barrier = pltpu.get_barrier_semaphore()
    inputs = [
        pltpu.make_async_copy(source, target, in_sem.at[i])
        for i, (source, target) in enumerate(
            [(slot_in, slot_ref), (off_in, off_ref), (tod_in, tod_ref),
             (ids_in, ids_ref), (prior_in, prior_ref)]
        )
    ]
    for copy in inputs:
        copy.start()

    @pl.loop(1, PLANE)
    def _(i):
        g, y = plane_peer(i)
        pl.semaphore_signal(barrier, inc=1, device_id={"grp": g, "rep": y}, device_id_type=MESH)

    @pl.loop(0, LINE - 1)
    def _(i):
        pl.semaphore_signal(
            barrier, inc=1, device_id={"blk": line_peer(i)}, device_id_type=MESH
        )

    for copy in inputs:
        copy.wait()

    @pl.loop(0, DET)
    def _(d):
        slot = slot_ref[pl.ds(d, 1), :]
        owner = slot // K
        place = (slot % K) * LINE + (owner % WINDOW) * COPIES + owner // WINDOW
        rows = lax.broadcasted_iota(jnp.int32, (LINE * K, SAMP), 0)
        s_hot[d] = jnp.where(rows == place, 1.0, 0.0).astype(BF16)
        rows = lax.broadcasted_iota(jnp.int32, (LANES, SAMP), 0)
        o_hot[d] = jnp.where(rows == off_ref[pl.ds(d, 1), :], 1.0, 0.0).astype(BF16)

    def local_map(first):
        acc[...] = jnp.zeros_like(acc)
        for d in range(DET):
            hot = o_hot[d]
            left = []
            for p in (first, first + 1):
                row = part[p, d : d + 1, :]
                left.append(hot * jnp.broadcast_to(row, (LANES, SAMP)).astype(BF16))
            acc[...] += lax.dot_general(
                jnp.concatenate(left, axis=0), s_hot[d],
                (((1,), (1,)), ((), ())), preferred_element_type=F32,
            )

    def send_map(f, image):
        for g in range(PLANE):
            for kh in range(2):
                psend[f, g, kh * SHARE : (kh + 1) * SHARE, :] = image[
                    g * SHARE : (g + 1) * SHARE, kh * LANES : (kh + 1) * LANES
                ]
        prec[f, me] = psend[f, me]
        plane_send(
            lambda g, y: psend.at[f, g * REPS + y], prec.at[f, me], ps_sem.at[f], pr_sem.at[f]
        )

    def to_owners(f):
        arrived(prec.at[f, pl.ds(0, PLANE - 1)], pr_sem.at[f])
        for l in range(LISTS_HERE):
            total = prec[f, l * REPS]
            for y in range(1, REPS):
                total = total + prec[f, l * REPS + y]
            tmp[0, l * 8 : l * 8 + 8, :] = total
        half = [
            [tmp[0, pl.ds(kh * SHARE + j, 8, stride=8), :] for kh in range(2)]
            for j in range(SHARE)
        ]
        lane = lanes_of((8, LANES))
        groups = []
        for kqh in range(2):
            for j in range(SHARE):
                for kql in range(2):
                    kq = kqh * 2 + kql
                    low = pltpu.roll(half[j][0], (-32 * kq) % LANES, 1)
                    high = pltpu.roll(half[j][1], (32 - 32 * kq) % LANES, 1)
                    groups.append(jnp.where(lane < 32, low, high))
        turned = jnp.transpose(jnp.concatenate(groups, axis=0))
        for w in range(WINDOW):
            for kh in range(2):
                start = kh * LINE + w * COPIES
                zsend[f, w, kh * COPIES : (kh + 1) * COPIES, :] = turned[start : start + COPIES]
        zrec[f, LINE // 2] = zsend[f, blk % WINDOW]
        line_send(
            lambda z: zsend.at[f, z % WINDOW],
            lambda z: zrec.at[f, line_slot(z)],
            zs_sem.at[f], zr_sem.at[f],
        )

    def line_slot(z):
        return (blk - z + LINE + LINE // 2) % LINE

    def at_owner(f, copy):
        rows = jnp.concatenate(
            [zrec[f, :, kh * COPIES + copy, :] for kh in range(2)], axis=0
        )
        both = jnp.concatenate([rows, pltpu.roll(rows, 64, 1)], axis=0)
        tmp[copy] = jnp.transpose(both)[:64]
        return jnp.concatenate(
            [tmp[copy, pl.ds(b, SHARE, stride=16), :] for b in range(16)], axis=1
        )

    def merged(f, count):
        arrived(zrec.at[f, pl.ds(0, LINE - 1)], zr_sem.at[f])
        totals = []
        for copy in range(COPIES):
            left = jnp.concatenate(pieces(at_owner(f, copy), count), axis=0)
            out = lax.dot_general(
                left, id_hot[copy], (((1,), (1,)), ((), ())), preferred_element_type=F32
            )
            total = out[:SHARE]
            for p in range(1, count):
                total = total + out[p * SHARE : (p + 1) * SHARE]
            totals.append(total)
        return jnp.concatenate(totals, axis=0)

    def near_lanes(shape):
        lane = lanes_of(shape)
        return lane // 64, (lane // ROWS) % WINDOW, (lane // COPIES) % 2, lane % COPIES

    def hot_ids():
        half, place, kh, copies = near_lanes((LANES, LANES))
        place = half * 64 + kh * LINE + LINE // 2 - WINDOW // 2 + place
        source = lax.broadcasted_iota(jnp.int32, (LANES, LANES), 0)
        near = jnp.zeros((16, LANES), F32)
        rows = lax.broadcasted_iota(jnp.int32, (256, LANES), 0)
        for copy in range(COPIES):
            ids = jnp.concatenate([idp[:, copy * 2 + kql, :] for kql in range(2)], axis=0)
            pick = jnp.where((source == place) & (copies == copy), 1.0, 0.0).astype(BF16)
            near = near + jnp.dot(ids.astype(BF16), pick, preferred_element_type=F32)
            ids = ids.astype(jnp.int32)
            for b in range(16):
                id_hot[copy, :, b * LANES : (b + 1) * LANES] = jnp.where(
                    rows == ids[b : b + 1], 1.0, 0.0
                ).astype(BF16)
        near = near.astype(jnp.int32)
        for b in range(16):
            near_hot[:, b * LANES : (b + 1) * LANES] = jnp.where(
                rows == near[b : b + 1], 1.0, 0.0
            ).astype(BF16)

    def send_back(b, values, count):
        left = jnp.concatenate(pieces(values, count), axis=0)
        out = jnp.dot(left, near_hot[...], preferred_element_type=F32)
        total = out[: COPIES * SHARE]
        for p in range(1, count):
            total = total + out[p * COPIES * SHARE : (p + 1) * COPIES * SHARE]
        copies = near_lanes((SHARE, LANES))[3]
        for c in range(16):
            chunk = total[:, c * LANES : (c + 1) * LANES]
            mine = chunk[:SHARE]
            for copy in range(1, COPIES):
                mine = jnp.where(copies == copy, chunk[copy * SHARE : (copy + 1) * SHARE], mine)
            tmp[0, pl.ds(c, SHARE, stride=16), :] = mine
        turned = jnp.transpose(
            jnp.concatenate([tmp[0], jnp.zeros((64, LANES), F32)], axis=0)
        )
        rows = jnp.where(
            lanes_of((64, LANES)) < 64, turned[:64], pltpu.roll(turned[64:], 64, 1)
        )
        for w in range(WINDOW):
            bsend[b, w] = rows[w * ROWS : (w + 1) * ROWS]
        brec[b, blk % WINDOW] = bsend[b, WINDOW // 2]
        near_send(
            lambda step: bsend.at[b, step + WINDOW // 2], brec.at[b, blk % WINDOW],
            bs_sem.at[b], br_sem.at[b],
        )

    def to_lists(b):
        arrived(brec.at[b, pl.ds(0, WINDOW - 1)], br_sem.at[b])
        rows = jnp.concatenate(
            [
                brec[b, w, kh * COPIES : (kh + 1) * COPIES, :]
                for kh in range(2)
                for w in range(WINDOW)
            ],
            axis=0,
        )
        turned = jnp.transpose(
            jnp.concatenate([rows, jnp.zeros((64, LANES), F32)], axis=0)
        )
        quarter = lanes_of((8, LANES)) // 32
        for j in range(SHARE):
            for kh in range(2):
                tile = jnp.zeros((8, LANES), F32)
                for kq in range(4):
                    start = (kq // 2) * 64 + j * 16 + (kq % 2) * 8
                    moved = pltpu.roll(
                        turned[start : start + 8], (32 * kq - 32 * kh) % LANES, 1
                    )
                    tile = jnp.where(quarter == kq, moved, tile)
                csend[b, pl.ds(kh * SHARE + j, 8, stride=8), :] = tile
        crec[b, me] = csend[b, pl.ds(pl.multiple_of(grp * 8, 8), 8), :]
        plane_send(
            lambda g, y: csend.at[b, pl.ds(pl.multiple_of(g * 8, 8), 8)],
            crec.at[b, me], cs_sem.at[b], cr_sem.at[b],
        )

    def picked(b, passes):
        arrived(crec.at[b, pl.ds(0, PLANE - 1)], cr_sem.at[b])
        for kh in range(2):
            for g in range(0, PLANE, 2):
                at = slice(kh * SHARE, (kh + 1) * SHARE)
                rows = jnp.concatenate([crec[b, g, at, :], crec[b, g + 1, at, :]], axis=0)
                acc[g * SHARE : g * SHARE + 8, kh * LANES : (kh + 1) * LANES] = rows
        for p, piece in enumerate(pieces(acc[:LANES, :], 3)):
            mt[p * LANES : (p + 1) * LANES, :] = piece
        yrow[...] = jnp.zeros_like(yrow)

        @pl.loop(0, passes)
        def _(q):
            left = mt[pl.ds(pl.multiple_of(q * 2 * LANES, 2 * LANES), 2 * LANES), :]
            for d in range(DET):
                out = jnp.dot(left, s_hot[d], preferred_element_type=F32)
                total = out[:LANES] + out[LANES:]
                yrow[d : d + 1, :] += jnp.sum(
                    total * o_hot[d].astype(F32), axis=0, keepdims=True
                )

        return folded(yrow[...])

    def tiles(value):
        return [value[:, t * LANES : (t + 1) * LANES] for t in range(TILES)]

    def folded(value):
        stacked = jnp.concatenate(tiles(value), axis=0)
        a = lax.broadcasted_iota(jnp.int32, (LANES, LANES), 0) // BL
        b = lanes_of((LANES, LANES)) // BL
        ones = jnp.where(a == b, 1.0, 0.0).astype(BF16)
        left = jnp.concatenate(pieces(stacked, 3), axis=0)
        out = jnp.dot(left, ones, preferred_element_type=F32)
        out = out[:64] + out[64:128] + out[128:]
        return jnp.concatenate([out[t * 8 : t * 8 + 8] for t in range(TILES)], axis=1)

    def smoothed(value):
        here = tiles(value)
        swapped = [pltpu.roll(t, 64, 1) for t in here]
        low = lanes_of((DET, LANES)) < 64
        odd = [jnp.where(low, swapped[t - 1], swapped[t]) for t in range(TILES)]
        spectrum = [
            jnp.broadcast_to(prior_ref[:, f : f + 1], (DET, LANES)) for f in range(BASES // 2 + 1)
        ]
        out = [jnp.zeros((DET, LANES), F32) for _ in range(TILES)]
        for shift in range(BASES):
            weight = jnp.zeros((DET, LANES), F32)
            for f in range(BASES // 2 + 1):
                share = (1.0 if f in (0, BASES // 2) else 2.0) / BASES
                weight = weight + spectrum[f] * (
                    share * math.cos(2.0 * math.pi * ((f * shift) % BASES) / BASES)
                )
            source = odd if shift % 2 else here
            for t in range(TILES):
                out[t] = out[t] + weight * source[(t - shift // 2) % TILES]
        return jnp.concatenate(out, axis=1)

    def lane_sums(value):
        total = functools.reduce(lambda a, b: a + b, tiles(value))
        total = jnp.sum(total, axis=0, keepdims=True)
        return total + pltpu.roll(total, 64, 1)

    rank = lax.broadcasted_iota(jnp.int32, (WINDOW, LINE), 0)
    owner = lanes_of((WINDOW, LINE))
    entry, lane = lax.broadcasted_iota(jnp.int32, (K, LANES), 0), lanes_of((K, LANES))
    listed = ids_ref[0].astype(F32).astype(BF16)
    row = jnp.zeros((WINDOW, LANES), F32)
    for copy in range(COPIES):
        pick = jnp.where(owner == copy * WINDOW + rank, 1.0, 0.0).astype(BF16)
        taken = jnp.dot(pick, listed, preferred_element_type=F32)
        pick = jnp.where(lane == copy * K + entry, 1.0, 0.0).astype(BF16)
        row = row + jnp.dot(taken.astype(BF16), pick, preferred_element_type=F32)
    idsend[...] = row.reshape(WINDOW, 1, LANES)

    def send_ids():
        idz[LINE // 2] = idsend[blk % WINDOW]
        line_send(
            lambda z: idsend.at[z % WINDOW], lambda z: idz.at[line_slot(z)],
            id_sem.at[0], id_sem.at[1],
        )

    def share_ids():
        arrived(idz.at[pl.ds(0, LINE - 1)], id_sem.at[1])
        rows = jnp.concatenate(
            [idz[...].reshape(LINE, LANES), jnp.zeros((LANES - LINE, LANES), F32)], axis=0
        )
        turned = jnp.transpose(rows)[: COPIES * K]
        quarter = lanes_of((4, LANES)) // LINE
        mine = jnp.zeros((4, LANES), F32)
        for kqh in range(2):
            for kh in range(2):
                some = [
                    turned[at : at + 1]
                    for copy in range(COPIES)
                    for kql in range(2)
                    for at in [copy * K + kh * 4 + kqh * 2 + kql]
                ]
                place = kqh * 2 + kh
                moved = pltpu.roll(jnp.concatenate(some, axis=0), place * LINE, 1)
                mine = jnp.where(quarter == place, moved, mine)
        idq[...] = mine
        idp[grp] = mine

        @pl.loop(1, LISTS_HERE)
        def _(i):
            g = ((grp // 2 + i // 2) % chips) * 2 + (grp % 2 + i % 2) % 2
            pltpu.make_async_remote_copy(
                src_ref=idq, dst_ref=idp.at[grp], send_sem=id_sem.at[2], recv_sem=id_sem.at[3],
                device_id={"grp": g}, device_id_type=MESH,
            ).start()

        arrived(idp.at[pl.ds(0, LISTS_HERE - 1)], id_sem.at[3])

    for p, piece in enumerate(pieces(tod_ref[...], 3)):
        part[p] = piece.astype(F32)
    part[3] = jnp.ones((DET, SAMP), F32)
    mt[3 * LANES :, :] = jnp.zeros((LANES, 256), BF16)
    for ref in (iterate, residual, direction, along):
        ref[...] = jnp.zeros_like(ref)
    for ref in (rr_ref, step_ref):
        ref[...] = jnp.ones_like(ref)
    low = lanes_of((1, LANES)) < 64

    @pl.loop(0, ROUNDS)
    def _(n):
        passes = jnp.where(n == 0, 2, 1)

        @pl.loop(0, passes)
        def _(q):
            local_map(2 * q)

            @pl.when(q == 0)
            def _():
                held[...] = acc[:LANES, :] + acc[LANES:, :]

            @pl.when(q == 1)
            def _():
                held[...] += acc[:LANES, :]

        @pl.when(n == 0)
        def _():
            pl.semaphore_wait(barrier, PLANE + LINE - 2)

        send_map(n, held[...])

        @pl.when(n == 0)
        def _():
            send_map(HITS, acc[LANES:, :])
            send_ids()
            rest[...] = folded(tod_ref[...])

        @pl.when(n > 0)
        def _():
            value = residual[...]
            image = BL * value + smoothed(value)
            rest[...] = image
            square = lane_sums(value * value) * (1.0 / BL)
            product = lane_sums(value * image) * (1.0 / BL)
            row = jnp.where(low, square, product)
            ssend[n] = row
            srec[n, me] = row
            plane_send(lambda g, y: ssend.at[n], srec.at[n, me], ss_sem.at[n], sr_sem.at[n])

        to_owners(n)

        @pl.when(n == 0)
        def _():
            to_owners(HITS)
            share_ids()
            hot_ids()
            divisor[...] = jnp.maximum(merged(HITS, 3), 1.0)

        @pl.when(n > 0)
        def _():
            arrived(srec.at[n, pl.ds(0, PLANE - 1)], sr_sem.at[n])
            row = jnp.sum(srec[n], axis=0)
            tsend[n] = row
            trec[n, blk] = row
            line_send(
                lambda z: tsend.at[n], lambda z: trec.at[n, blk], ts_sem.at[n], tr_sem.at[n]
            )

        sums = merged(n, 3)
        binned = sums / divisor[...]
        send_back(n, binned, 3)

        @pl.when(n > 0)
        def _():
            energy = jnp.sum(sums * binned, axis=0, keepdims=True)
            row = energy[:, :LANES] + energy[:, LANES:]
            wsend[n] = row
            wrec[n, blk % WINDOW] = row
            near_send(
                lambda step: wsend.at[n], wrec.at[n, blk % WINDOW], ws_sem.at[n], wr_sem.at[n]
            )

        to_lists(n)

        @pl.when(n > 0)
        def _():
            arrived(wrec.at[n, pl.ds(0, WINDOW - 1)], wr_sem.at[n])
            row = jnp.sum(wrec[n], axis=0)
            usend[n] = row
            urec[n, me] = row
            plane_send(lambda g, y: usend.at[n], urec.at[n, me], us_sem.at[n], ur_sem.at[n])

        image = rest[...] - picked(n, passes)

        @pl.when(n == 0)
        def _():
            residual[...] = image

        @pl.when(n > 0)
        def _():
            arrived(trec.at[n, pl.ds(0, LINE - 1)], tr_sem.at[n])
            arrived(urec.at[n, pl.ds(0, PLANE - 1)], ur_sem.at[n])
            row = jnp.sum(trec[n], axis=0)
            energy = jnp.sum(jnp.sum(urec[n], axis=0), axis=1, keepdims=True)
            new = jnp.sum(jnp.where(low, row, 0.0), axis=1, keepdims=True)
            curve = jnp.sum(jnp.where(low, 0.0, row), axis=1, keepdims=True) - energy
            ratio = jnp.where(n == 1, 0.0, new / rr_ref[:, 0:1])
            step = new / (curve - ratio * new / step_ref[:, 0:1])
            rr_ref[...] = jnp.broadcast_to(new, (1, LANES))
            step_ref[...] = jnp.broadcast_to(step, (1, LANES))
            course = residual[...] + ratio * direction[...]
            change = image + ratio * along[...]
            direction[...] = course
            along[...] = change
            iterate[...] += step * course
            residual[...] -= step * change

        for p, piece in enumerate(pieces(residual[...], 2)):
            part[p] = piece.astype(F32)

    for ref, value in ((x_ref, iterate[...]), (r_ref, residual[...])):
        out = jnp.zeros((DET, LANES), F32)
        lane = lanes_of((DET, LANES))
        for t, tile in enumerate(tiles(value)):
            for side in range(2):
                spread = jnp.broadcast_to(tile[:, side * BL : side * BL + 1], (DET, LANES))
                out = jnp.where(lane == 2 * t + side, spread, out)
        ref[...] = out[:, :BASES]

    arrived(idz.at[pl.ds(0, LINE - 1)], id_sem.at[0])
    arrived(idp.at[pl.ds(0, LISTS_HERE - 1)], id_sem.at[2])
    for f in range(OUT):
        arrived(prec.at[f, pl.ds(0, PLANE - 1)], ps_sem.at[f])
        arrived(zrec.at[f, pl.ds(0, LINE - 1)], zs_sem.at[f])
    for b in range(ROUNDS):
        arrived(brec.at[b, pl.ds(0, WINDOW - 1)], bs_sem.at[b])
        arrived(crec.at[b, pl.ds(0, PLANE - 1)], cs_sem.at[b])
    for n in range(1, ROUNDS):
        arrived(srec.at[n, pl.ds(0, PLANE - 1)], ss_sem.at[n])
        arrived(trec.at[n, pl.ds(0, LINE - 1)], ts_sem.at[n])
        arrived(wrec.at[n, pl.ds(0, WINDOW - 1)], ws_sem.at[n])
        arrived(urec.at[n, pl.ds(0, PLANE - 1)], us_sem.at[n])


def shards(tod, hit_ids, sample_slot, sample_offset, prior):
    whole = pl.BlockSpec(memory_space=pltpu.VMEM)
    dma = pltpu.SemaphoreType.DMA
    return pl.pallas_call(
        kernel,
        out_shape=[jax.ShapeDtypeStruct((DET, BASES), F32)] * 2,
        in_specs=[pl.BlockSpec(memory_space=pl.ANY)] * 5,
        out_specs=[whole] * 2,
        scratch_shapes=[
            pltpu.VMEM((1, LINE, K), jnp.int32),
            pltpu.VMEM((DET, SAMP), F32),
            pltpu.VMEM((DET, SAMP), jnp.int32),
            pltpu.VMEM((DET, SAMP), jnp.int32),
            pltpu.VMEM((DET, BASES // 2 + 1), F32),
            dma((5,)),
            pltpu.VMEM((WINDOW, 1, LANES), F32),
            pltpu.VMEM((LINE, 1, LANES), F32),
            pltpu.VMEM((4, LANES), F32),
            pltpu.VMEM((LISTS_HERE, 4, LANES), F32),
            dma((4,)),
            pltpu.VMEM((DET, SAMP), F32),
            pltpu.VMEM((DET, SAMP), F32),
            pltpu.VMEM((DET, SAMP), F32),
            pltpu.VMEM((DET, SAMP), F32),
            pltpu.VMEM((DET, SAMP), F32),
            pltpu.VMEM((LANES, 256), F32),
            pltpu.VMEM((COPIES * SHARE, 256), F32),
            pltpu.VMEM((1, LANES), F32),
            pltpu.VMEM((1, LANES), F32),
            pltpu.VMEM((DET, LINE * K, SAMP), BF16),
            pltpu.VMEM((DET, LANES, SAMP), BF16),
            pltpu.VMEM((COPIES, 256, LINE * LISTS_HERE * K), BF16),
            pltpu.VMEM((256, LINE * LISTS_HERE * K), BF16),
            pltpu.VMEM((256, 256), F32),
            pltpu.VMEM((4, DET, SAMP), F32),
            pltpu.VMEM((COPIES, 64, LANES), F32),
            pltpu.VMEM((4 * LANES, 256), BF16),
            pltpu.VMEM((DET, SAMP), F32),
            pltpu.VMEM((OUT, PLANE, 8, LANES), F32),
            pltpu.VMEM((OUT, PLANE, 8, LANES), F32),
            pltpu.VMEM((OUT, WINDOW, ROWS, LANES), F32),
            pltpu.VMEM((OUT, LINE, ROWS, LANES), F32),
            pltpu.VMEM((ROUNDS, WINDOW, ROWS, LANES), F32),
            pltpu.VMEM((ROUNDS, WINDOW, ROWS, LANES), F32),
            pltpu.VMEM((ROUNDS, 64, LANES), F32),
            pltpu.VMEM((ROUNDS, PLANE, 8, LANES), F32),
            pltpu.VMEM((ROUNDS, 1, LANES), F32),
            pltpu.VMEM((ROUNDS, PLANE, 1, LANES), F32),
            pltpu.VMEM((ROUNDS, 1, LANES), F32),
            pltpu.VMEM((ROUNDS, LINE, 1, LANES), F32),
            pltpu.VMEM((ROUNDS, 1, LANES), F32),
            pltpu.VMEM((ROUNDS, WINDOW, 1, LANES), F32),
            pltpu.VMEM((ROUNDS, 1, LANES), F32),
            pltpu.VMEM((ROUNDS, PLANE, 1, LANES), F32),
        ]
        + [dma((OUT,))] * 4 + [dma((ROUNDS,))] * 4 + [dma((ROUNDS,))] * 8,
        compiler_params=pltpu.CompilerParams(
            collective_id=0, has_side_effects=True, vmem_limit_bytes=40 * 1024 * 1024
        ),
    )(hit_ids, tod, sample_slot, sample_offset, prior)


def solution(mesh):
    rows = P(("grp", "blk", "rep"), None)
    return jax.shard_map(
        shards,
        mesh=mesh,
        in_specs=(rows, P(("grp", "blk"), None, None), rows, rows, rows),
        out_specs=(rows, rows),
        check_vma=False,
    )
```

time: 215 us -> 184 us (0.86)
  Pallas kernels: 209 us -> 179 us
    pallas_call x1, Pallas kernels: 209 us -> 179 us  [shards(): pl.pallas_call(kernel, out_shape=[jax.ShapeDtypeStruct((DET, BASES), F32)...]
where the time goes in v2:
time: 184 us
  Pallas kernels  179 us (97%)
  local copies, waits for them, and re-layouts  4.23 us (2%)
    pallas_call x1, Pallas kernels, shards(): pl.pallas_call(kernel, out_shape=[jax.ShapeDtypeStruct((DET, BASES), F32)...  179 us
    unnamed x11, local copies, waits for them, and re-layouts  4.23 us

profile of v2, /device:TPU:1, one launch (start us, length us, event | category | flops | bytes accessed | tf_op | source)
XLA Modules:
  0.0 183.7 jit_solution(11105011205882410912)
XLA Ops:
  0.6 0.0 copy-start.3
  0.6 0.8 copy.7.ids_in
  1.4 0.0 copy-done.3
  1.4 0.0 copy-start
  1.4 0.8 copy-done
  2.2 0.0 copy-start.1
  2.2 0.8 copy-done.1
  2.9 0.0 copy-start.2
  2.9 0.8 copy-done.2
  3.7 178.8 %shard_map.68 = (f32[8,16]{1,0:T(8,128)S(1)}, f32[8,16]{1,0:T(8,128)S(1)}) custom-call(s32[1,32,8]{2,1,0:T(8,128)S(1)} %copy.7.ids_in, f32[8,1024]{1,0:T(8,128)S(1)} %copy-done, s32[8,1024]{1,0:T(8,128)S(1)} %copy-done.1, s32[8,1024]{1,0:T(8,128)S(1)} %copy-done.2, f32[8,9]{1,0:T(8,128)S(1)} %copy-done.3), custom_call_target="tpu_custom_call" | custom-call | tf_op jit(solution)/shard_map/pallas_call | solution.py:570
  182.5 0.6 copy.10
  183.1 0.6 copy.11
Async XLA Ops:
  0.6 0.8 copy-start.3
  1.4 0.8 copy-start
  2.2 0.8 copy-start.1
  2.9 0.8 copy-start.2
